TPU v7x, 256 devices: a whole 4x4x8 slice. The times are simulated.
256 devices in a mesh: dom: 8 (over z), row: 16 (over y, x), col: 2 (over core).
Axes of the slice: x: 4, y: 4, z: 8, core: 2. Of those that a mesh axis runs over, the one named last changes fastest.
Arguments:
- next_inverse: bfloat16 [8, 4096, 4096], P('dom', 'row', 'col'), may hold values from -6 to 6
- next_arrow: bfloat16 [8, 64, 4096], P('dom', None, 'row'), may hold values from -6 to 6
- factor_win: bfloat16 [8, 4096, 3072], P('dom', 'row', 'col'), may hold values from -0.09375 to 0.09375
- factor_rest: bfloat16 [8, 4096, 1024], P('dom', 'row', 'col'), may hold values from -0.09375 to 0.09375
- arrow_win: bfloat16 [8, 64, 3072], P('dom', None, 'col'), may hold values from -0.75 to 0.75
- arrow_rest: bfloat16 [8, 64, 1024], P('dom', None, 'col'), may hold values from -0.75 to 0.75
- tip_inverse: bfloat16 [64, 64], replicated, may hold values from -6 to 6
- base_win: bfloat16 [8, 3072, 3072], P('dom', 'row', 'col'), may hold values from -6 to 6
- base_rest: bfloat16 [8, 3072, 1024], P('dom', 'row', 'col'), may hold values from -6 to 6
Outputs:
- sub_inverse: bfloat16 [8, 4096, 3072], P('dom', 'row', 'col')
- arrow_inverse: bfloat16 [8, 64, 3072], P('dom', None, 'col')
- diag_win: bfloat16 [8, 3072, 3072], P('dom', 'row', 'col')
- diag_rest: bfloat16 [8, 3072, 1024], P('dom', 'row', 'col')
All inputs are finite; a program needn't handle non-finite values.
Results may differ from a plain program's by a relative error of at most 0.0046.
Values may be sent and summed in bfloat16 or wider, within the bound.
A program may use at most 128 MiB of HBM per device.

v0:
```python
import jax
import jax.numpy as jnp
from jax import lax
from jax.sharding import PartitionSpec as P


def shifted(value, axis, steps):
    count = lax.axis_size(axis)
    leading, last = (max(0, -steps), min(count, count - steps))
    return lax.ppermute(value, axis, [(source, source + steps) for source in range(leading, last)])


def contract_first(left, right):
    return lax.dot_general(
        left, right, (((0,), (0,)), ((), ())), preferred_element_type=jnp.float32
    )


def per_device(
    next_inverse,
    next_arrow,
    factor_win,
    factor_rest,
    arrow_win,
    arrow_rest,
    tip_inverse,
    base_win,
    base_rest,
):
    inverse_tile = next_inverse[0]
    arrow_tile = next_arrow[0]
    factor_tile = factor_win[0]
    factor_other = factor_rest[0]
    ratio_tile = arrow_win[0]
    ratio_other = arrow_rest[0]
    factor_column = lax.all_gather(factor_tile, "row", axis=0, tiled=True)
    inverse_next, arrow_next = shifted((inverse_tile, arrow_tile), "dom", -1)
    start_sum = contract_first(arrow_next, ratio_tile)
    x_total = start_sum + jnp.dot(
        lax.all_gather(inverse_next, "col", axis=1, tiled=True),
        factor_column,
        preferred_element_type=jnp.float32,
    )
    x_bf = x_total.astype(jnp.bfloat16)
    y_part = jnp.dot(arrow_next, factor_tile, preferred_element_type=jnp.float32)
    y_total = lax.psum(y_part, "row") + jnp.dot(
        tip_inverse, ratio_tile, preferred_element_type=jnp.float32
    )
    y_bf = y_total.astype(jnp.bfloat16)
    x_panel, y_panel = (
        lax.all_gather(x_bf, "col", axis=1, tiled=True),
        lax.all_gather(y_bf, "col", axis=1, tiled=True),
    )
    ratio_both = jnp.concatenate([ratio_tile, ratio_other], axis=1)
    rows_here = y_panel.shape[1] // lax.axis_size("row")
    y_rows = lax.dynamic_slice_in_dim(y_panel, lax.axis_index("row") * rows_here, rows_here, 1)
    x_columns = lax.all_to_all(x_panel, "row", split_axis=1, concat_axis=0, tiled=True)
    rest_column = lax.all_gather(factor_other, "row", axis=0, tiled=True)
    factor_full = jnp.concatenate([factor_column, rest_column], axis=1)
    diag_part = contract_first(x_columns, factor_full)
    base_both = jnp.concatenate([base_win[0], base_rest[0]], axis=1).astype(jnp.float32)
    diag_total = base_both + diag_part + contract_first(y_rows, ratio_both)
    split = factor_tile.shape[1]
    diag_left = diag_total[:, :split].astype(jnp.bfloat16)
    diag_right = diag_total[:, split:].astype(jnp.bfloat16)
    return ((-x_bf)[None], (-y_bf)[None], diag_left[None], diag_right[None])


def solution(mesh):
    in_specs = (
        P("dom", "row", "col"),
        P("dom", None, "row"),
        P("dom", "row", "col"),
        P("dom", "row", "col"),
        P("dom", None, "col"),
        P("dom", None, "col"),
        P(),
        P("dom", "row", "col"),
        P("dom", "row", "col"),
    )
    out_specs = (
        P("dom", "row", "col"),
        P("dom", None, "col"),
        P("dom", "row", "col"),
        P("dom", "row", "col"),
    )
    return jax.shard_map(
        per_device, mesh=mesh, in_specs=in_specs, out_specs=out_specs, check_vma=False
    )
```

profile of v0, /device:TPU:1, one launch (start us, length us, event | category | flops | bytes accessed | tf_op | source)
XLA Modules:
  0.0 360.3 jit_solution(10407591954021950761)
XLA Ops:
  7.2 1.3 collective-permute-start.1
  8.5 24.2 %collective-permute-done.1 = bf16[256,2048]{1,0:T(8,128)(2,1)S(1)} collective-permute-done((bf16[256,2048]{1,0:T(8,128)(2,1)}, bf16[256,2048]{1,0:T(8,128)(2,1)S(1)}, u32[]{:S(2)}, u32[]{:S(2)}) %collective-permute-start.1) | collective-permute-done | bytes 1048608 | tf_op jit(solution)/shard_map/ppermute | solution.py:10
  32.8 1.0 copy-done.4
  33.9 0.7 all-gather.11.cloned.1.call-update
  34.6 1.4 collective-permute-start
  36.1 19.8 %all-gather.7.cloned.1.call-done = bf16[256,4096]{1,0:T(8,128)(2,1)} async-done(((bf16[256,2048]{1,0:T(8,128)(2,1)}), bf16[256,4096]{1,0:T(8,128)(2,1)}) %all-gather.7.cloned.1.call-update) | async-done | bytes 2097168 | tf_op jit(solution)/shard_map/all_gather | solution.py:40
  55.9 98.0 %all-gather.11.cloned.1.call-done = bf16[1,4096,1536]{2,1,0:T(8,128)(2,1)} async-done(((bf16[1,256,1536]{2,1,0:T(8,128)(2,1)}), bf16[1,4096,1536]{2,1,0:T(8,128)(2,1)}) %all-gather.11.cloned.1.call-update) | async-done | bytes 12582928 | tf_op jit(solution)/shard_map/all_gather | solution.py:36
  153.9 7.0 %fusion.18 = f32[256,1536]{1,0:T(8,128)S(1)} fusion(bf16[256,4096]{1,0:T(8,128)(2,1)} %all-gather.7.cloned.1.call-done, bf16[1,4096,1536]{2,1,0:T(8,128)(2,1)} %all-gather.11.cloned.1.call-done), kind=kOutput, calls=%fused_computation.23 | convolution fusion | flops 3221225472 | bytes 16252928 | tf_op jit(solution)/shard_map/dot_general | solution.py:39
  161.0 1.3 fusion.4
  162.3 1.0 fusion.9
  163.4 0.5 all-gather.13.cloned.1.call-update
  163.9 14.1 %all-gather.9.cloned.1.call-done = bf16[256,3072]{1,0:T(8,128)(2,1)} async-done(((bf16[256,1536]{1,0:T(8,128)(2,1)}), bf16[256,3072]{1,0:T(8,128)(2,1)}) %all-gather.9.cloned.1.call-update) | async-done | bytes 1572880 | tf_op jit(solution)/shard_map/all_gather | solution.py:51
  178.0 2.6 copy.13
  180.6 6.3 %all-to-all-start = ((bf16[256,16,192]{0,2,1:T(8,128)(2,1)}), bf16[256,16,192]{0,2,1:T(8,128)(2,1)S(1)}, u32[]{:S(2)}, u32[]{:S(2)}) async-start(bf16[256,16,192]{0,2,1:T(8,128)(2,1)} %bitcast.9), calls=%async_computation | async-start | bytes 3145728 | tf_op jit(solution)/shard_map/all_to_all | solution.py:57
  186.9 0.2 fusion.20
  187.1 95.9 %all-reduce.2.cloned.1.call-done = f32[64,1536]{1,0:T(8,128)} async-done(((f32[64,1536]{1,0:T(8,128)}), f32[64,1536]{1,0:T(8,128)}) %all-reduce.2.cloned.1.call-update) | async-done | bytes 393232 | tf_op jit(solution)/shard_map/psum | solution.py:46
  283.0 1.7 negate_bitcast_fusion.1
  284.7 3.8 %all_gather.19 = bf16[64,3072]{1,0:T(8,128)(2,1)} all-gather(bf16[64,1536]{1,0:T(8,128)(2,1)S(1)} %get-tuple-element.5), channel_id=1, replica_groups=mesh['dom'=8,'row'=16,'col'=2] {'col'}, dimensions={1}, use_global_device_ids=true | all-gather | bytes 589824 | tf_op jit(solution)/shard_map/all_gather | solution.py:52
  288.5 0.9 negate_bitcast_fusion
  289.6 53.0 %all-gather.13.cloned.1.call-done = bf16[1,4096,512]{2,1,0:T(8,128)(2,1)} async-done(((bf16[1,256,512]{2,1,0:T(8,128)(2,1)}), bf16[1,4096,512]{2,1,0:T(8,128)(2,1)}) %all-gather.13.cloned.1.call-update) | async-done | bytes 4194320 | tf_op jit(solution)/shard_map/all_gather | solution.py:58
  342.6 8.4 %fusion.5 = f32[192,2048]{1,0:T(8,128)S(1)} fusion(bf16[4096,192]{0,1:T(8,128)(2,1)S(1)} %bitcast.36, bf16[4096,512]{1,0:T(8,128)(2,1)} %bitcast.39, bf16[4096,1536]{1,0:T(8,128)(2,1)} %bitcast.38, bf16[192,512]{1,0:T(8,128)(2,1)S(1)} %bitcast.42, bf16[192,1536]{1,0:T(8,128)(2,1)} %bitcast.41), kind=kOutput, calls=%fused_computation.7 | convolution fusion | flops 3256745984 | bytes 20709376 | tf_op jit(solution)/shard_map/dot_general | solution.py:14
  351.0 1.3 fusion.8
  352.2 0.9 slice_bitcast_fusion
  353.1 0.7 slice_bitcast_fusion.1
  (26 shorter events, 0.5 us)
Async XLA Ops:
  7.2 179.7 %copy-start = (bf16[64,64]{1,0:T(8,128)(2,1)S(1)}, bf16[64,64]{1,0:T(8,128)(2,1)}, u32[]{:S(2)}) copy-start(bf16[64,64]{1,0:T(8,128)(2,1)} %param.15) | copy-start | bytes 24580
  7.2 27.4 %copy-start.7 = (bf16[1,64,256]{2,1,0:T(8,128)(2,1)S(1)}, bf16[1,64,256]{2,1,0:T(8,128)(2,1)}, u32[]{:S(2)}) copy-start(bf16[1,64,256]{2,1,0:T(8,128)(2,1)} %param.10) | copy-start | bytes 98308
  7.2 48.7 %all-gather.7.cloned.1.call-start = ((), (), s32[]{:S(2)}) async-start(), calls=%async_computation.1 | async-start | bytes 3145728 | tf_op jit(solution)/shard_map/all_gather | solution.py:40
  7.2 25.5 %collective-permute-start.1 = (bf16[256,2048]{1,0:T(8,128)(2,1)}, bf16[256,2048]{1,0:T(8,128)(2,1)S(1)}, u32[]{:S(2)}, u32[]{:S(2)}) collective-permute-start(bf16[256,2048]{1,0:T(8,128)(2,1)} %bitcast.40), channel_id=1, source_target_pairs={{32,0},{64,32},{96,64},{128,96},{160,128},{192,160},{224,192},{33,... | collective-permute-start | bytes 3145736 | tf_op jit(solution)/shard_map/ppermute | solution.py:10
  32.8 1.0 copy-start.4
  33.8 120.1 %all-gather.11.cloned.1.call-start = ((), (), s32[]{:S(2)}) async-start(), calls=%async_computation.4 | async-start | bytes 13369344 | tf_op jit(solution)/shard_map/all_gather | solution.py:36
  34.6 143.5 %all-gather.9.cloned.1.call-start = ((), (), s32[]{:S(2)}) async-start(), calls=%async_computation.3 | async-start | bytes 2359296 | tf_op jit(solution)/shard_map/all_gather | solution.py:51
  34.6 126.3 %copy-start.3 = (bf16[1,64,1536]{2,1,0:T(8,128)(2,1)S(1)}, bf16[1,64,1536]{2,1,0:T(8,128)(2,1)}, u32[]{:S(2)}) copy-start(bf16[1,64,1536]{2,1,0:T(8,128)(2,1)} %param.13) | copy-start | bytes 589828
  34.6 126.3 %collective-permute-start = (bf16[64,256]{1,0:T(8,128)(2,1)S(1)}, bf16[64,256]{1,0:T(8,128)(2,1)S(1)}, u32[]{:S(2)}, u32[]{:S(2)}) collective-permute-start(bf16[64,256]{1,0:T(8,128)(2,1)S(1)} %bitcast.43), channel_id=1, source_target_pairs={{32,0},{64,32},{96,64},{128,96},{160,128},{192,160},{224,192},{33,... | collective-permute-start | bytes 98312 | tf_op jit(solution)/shard_map/ppermute | solution.py:10
  160.9 1.4 copy-start.2
  162.3 120.7 %all-reduce.2.cloned.1.call-start = ((), (), s32[]{:S(2)}) async-start(), calls=%async_computation.2 | async-start | bytes 786432 | tf_op jit(solution)/shard_map/psum | solution.py:46
  163.3 179.2 %all-gather.13.cloned.1.call-start = ((), (), s32[]{:S(2)}) async-start(), calls=%async_computation.5 | async-start | bytes 4456448 | tf_op jit(solution)/shard_map/all_gather | solution.py:58
  180.6 108.8 %all-to-all-start = ((bf16[256,16,192]{0,2,1:T(8,128)(2,1)}), bf16[256,16,192]{0,2,1:T(8,128)(2,1)S(1)}, u32[]{:S(2)}, u32[]{:S(2)}) async-start(bf16[256,16,192]{0,2,1:T(8,128)(2,1)} %bitcast.9), calls=%async_computation | async-start | bytes 3145728 | tf_op jit(solution)/shard_map/all_to_all | solution.py:57
  186.9 101.6 %copy-start.1 = (bf16[256,1536]{1,0:T(8,128)(2,1)S(1)}, bf16[256,1536]{1,0:T(8,128)(2,1)}, u32[]{:S(2)}) copy-start(bf16[256,1536]{1,0:T(8,128)(2,1)} %fusion.4) | copy-start | bytes 2359300
  289.4 53.1 %copy-start.6 = (bf16[1,192,512]{2,1,0:T(8,128)(2,1)S(1)}, bf16[1,192,512]{2,1,0:T(8,128)(2,1)}, u32[]{:S(2)}) copy-start(bf16[1,192,512]{2,1,0:T(8,128)(2,1)} %param.17) | copy-start | bytes 589828
  342.6 8.4 %copy-start.5 = (bf16[1,64,512]{2,1,0:T(8,128)(2,1)S(1)}, bf16[1,64,512]{2,1,0:T(8,128)(2,1)}, u32[]{:S(2)}) copy-start(bf16[1,64,512]{2,1,0:T(8,128)(2,1)} %param.14) | copy-start | bytes 196612
Sparse Core Ops, SparseCore 0:
  33.9 21.8 all-gather.6
  58.3 95.5 all-gather.10
  162.4 15.6 all-gather.8
  181.7 101.2 all-reduce.1
  285.3 57.2 all-gather.12
where the time goes:
time: 361 us; the launch traced here: 360 us
  waiting for transfers between devices  306 us (85%)
  matrix products  19.1 us (5%)
  between operations  13.9 us (4%)
  starting transfers between devices  9.18 us (3%)
  local copies, waits for them, and re-layouts  5.35 us (1%)
  blocking collectives  3.8 us (1%)
    all_gather x1, waiting for transfers between devices, per_device(): factor_column = lax.all_gather(factor_tile, 'row', axis=0, tiled=True)  98 us
    psum x1, waiting for transfers between devices, per_device(): lax.psum(y_part, 'row')  95.9 us
    all_gather x1, waiting for transfers between devices, per_device(): rest_column = lax.all_gather(factor_other, 'row', axis=0, tiled=True)  53 us
    ppermute x2, waiting for transfers between devices, shifted(): lax.ppermute(value, axis, [(source, source + steps) for source in range(l...  24.2 us
    all_gather x1, waiting for transfers between devices, per_device(): lax.all_gather(inverse_next, 'col', axis=1, tiled=True)  19.8 us
    all_gather x1, waiting for transfers between devices, per_device(): lax.all_gather(x_bf, 'col', axis=1, tiled=True)  14.1 us
    dot_general x3, matrix products, contract_first(): lax.dot_general(left, right, (((0,), (0,)), ((), ())), preferred_element_...  10.9 us
  transfers between devices with their start and end apart: 8, of which 6 were waited for; matrix products, arithmetic and copies ran while one was open for 4% of the time, Pallas kernels for 0%

commit v1 on v0

--- a/solution.py
+++ b/solution.py
@@ -55,7 +55,30 @@
     rows_here = y_panel.shape[1] // lax.axis_size("row")
     y_rows = lax.dynamic_slice_in_dim(y_panel, lax.axis_index("row") * rows_here, rows_here, 1)
     x_columns = lax.all_to_all(x_panel, "row", split_axis=1, concat_axis=0, tiled=True)
-    rest_column = lax.all_gather(factor_other, "row", axis=0, tiled=True)
+    plain, t_next, response = (lax.axis_size("row"), lax.axis_index("row"), factor_other.shape[0])
+    trail = [(c, (c + 1) % plain) for c in range(plain)]
+    chunks = [(c, (c - 1) % plain) for c in range(plain)]
+    rest_column = jnp.zeros(
+        (*factor_other.shape[:0], plain * response, *factor_other.shape[0 + 1 :]),
+        factor_other.dtype,
+    )
+    rest_column = lax.dynamic_update_slice_in_dim(
+        rest_column, factor_other, t_next * response, axis=0
+    )
+    work_now = z2 = factor_other
+    x_now = plain // 2
+    kk = 1
+    while kk < x_now + 1:
+        work_now = lax.ppermute(work_now, axis_name="row", perm=trail)
+        rest_column = lax.dynamic_update_slice_in_dim(
+            rest_column, work_now, (t_next - kk) % plain * response, axis=0
+        )
+        if kk < plain - x_now:
+            z2 = lax.ppermute(z2, axis_name="row", perm=chunks)
+            rest_column = lax.dynamic_update_slice_in_dim(
+                rest_column, z2, (t_next + kk) % plain * response, axis=0
+            )
+        kk = kk + 1
     factor_full = jnp.concatenate([factor_column, rest_column], axis=1)
     diag_part = contract_first(x_columns, factor_full)
     base_both = jnp.concatenate([base_win[0], base_rest[0]], axis=1).astype(jnp.float32)

time: 361 us -> 342 us (0.947)
  waiting for transfers between devices: 306 us -> 237 us
  starting transfers between devices: 9.18 us -> 41.6 us
  local copies, waits for them, and re-layouts: 5.35 us -> 20 us
    all_gather x1 -> x0, waiting for transfers between devices: 53 us -> none  [per_device(): rest_column = lax.all_gather(factor_other, 'row', axis=0, tiled=True)]
    ppermute x0 -> x15, starting transfers between devices: none -> 32.6 us  [the longest x7 29.5 us: per_device(): z2 = lax.ppermute(z2, axis_name='row', perm=chunks)]
    ppermute x0 -> x15, waiting for transfers between devices: none -> 30.3 us  [the longest x7 18.7 us: per_device(): z2 = lax.ppermute(z2, axis_name='row', perm=chunks)]
    all_gather x1, waiting for transfers between devices: 19.8 us -> 0.07 us  [per_device(): lax.all_gather(inverse_next, 'col', axis=1, tiled=True)]
    all_gather x1, waiting for transfers between devices: 14.1 us -> 0.01 us  [per_device(): lax.all_gather(x_bf, 'col', axis=1, tiled=True)]
    psum x1, waiting for transfers between devices: 95.9 us -> 83.3 us  [per_device(): lax.psum(y_part, 'row')]
    dynamic_update_slice x0 -> x16, local copies, waits for them, and re-layouts: none -> 12.5 us  [the longest x8 6.69 us: per_device(): lax.dynamic_update_slice_in_dim(rest_column, work_now, (t_next - kk) % pl...]
  transfers between devices with their start and end apart: 8 -> 22, of which waited for: 6 -> 11; matrix products, arithmetic and copies ran while one was open for 4% -> 10% of each run, Pallas kernels for 0% -> 0%
where the time goes in v1:
time: 342 us; the launch traced here: 341 us
  waiting for transfers between devices  237 us (69%)
  starting transfers between devices  41.6 us (12%)
  matrix products  22 us (6%)
  local copies, waits for them, and re-layouts  20 us (6%)
  between operations  13.9 us (4%)
  blocking collectives  3.67 us (1%)
    all_gather x1, waiting for transfers between devices, per_device(): factor_column = lax.all_gather(factor_tile, 'row', axis=0, tiled=True)  98 us
    psum x1, waiting for transfers between devices, per_device(): lax.psum(y_part, 'row')  83.3 us
    ppermute x7, starting transfers between devices, per_device(): z2 = lax.ppermute(z2, axis_name='row', perm=chunks)  29.5 us
    ppermute x2, waiting for transfers between devices, shifted(): lax.ppermute(value, axis, [(source, source + steps) for source in range(l...  24.2 us
    ppermute x7, waiting for transfers between devices, per_device(): z2 = lax.ppermute(z2, axis_name='row', perm=chunks)  18.7 us
    dot_general x3, matrix products, contract_first(): lax.dot_general(left, right, (((0,), (0,)), ((), ())), preferred_element_...  11.7 us
    ppermute x8, waiting for transfers between devices, per_device(): work_now = lax.ppermute(work_now, axis_name='row', perm=trail)  11.5 us
    dot_general x1, matrix products, per_device(): jnp.dot(lax.all_gather(inverse_next, 'col', axis=1, tiled=True), factor_c...  7.05 us
  transfers between devices with their start and end apart: 22, of which 11 were waited for; matrix products, arithmetic and copies ran while one was open for 10% of the time, Pallas kernels for 0%

profile of v1, /device:TPU:1, one launch (start us, length us, event | category | flops | bytes accessed | tf_op | source)
XLA Modules:
  0.0 340.5 jit_solution(9944222487709581829)
XLA Ops:
  8.5 24.2 %collective-permute-done.1 = bf16[256,2048]{1,0:T(8,128)(2,1)S(1)} collective-permute-done((bf16[256,2048]{1,0:T(8,128)(2,1)}, bf16[256,2048]{1,0:T(8,128)(2,1)S(1)}, u32[]{:S(2)}, u32[]{:S(2)}) %collective-permute-start.1) | collective-permute-done | bytes 1048608 | tf_op jit(solution)/shard_map/ppermute | solution.py:10
  34.6 3.1 collective-permute-start.2
  37.7 3.8 %collective-permute-start.3 = (bf16[256,512]{1,0:T(8,128)(2,1)}, bf16[256,512]{1,0:T(8,128)(2,1)S(1)}, u32[]{:S(2)}, u32[]{:S(2)}) collective-permute-start(bf16[256,512]{1,0:T(8,128)(2,1)} %bitcast.40), channel_id=1, source_target_pairs={{0,30},{2,0},{4,2},{6,4},{8,6},{10,8},{12,10},{14,12},{16,14},{18,... | collective-permute-start | bytes 786440 | tf_op jit(solution)/shard_map/ppermute | solution.py:77
  42.8 4.0 %collective-permute-done.2 = bf16[256,512]{1,0:T(8,128)(2,1)S(1)} collective-permute-done((bf16[256,512]{1,0:T(8,128)(2,1)}, bf16[256,512]{1,0:T(8,128)(2,1)S(1)}, u32[]{:S(2)}, u32[]{:S(2)}) %collective-permute-start.2) | collective-permute-done | bytes 262176 | tf_op jit(solution)/shard_map/ppermute | solution.py:72
  47.9 2.1 fusion.14
  50.1 4.9 %collective-permute-start.5 = (bf16[256,512]{1,0:T(8,128)(2,1)S(1)}, bf16[256,512]{1,0:T(8,128)(2,1)S(1)}, u32[]{:S(2)}, u32[]{:S(2)}) collective-permute-start(bf16[256,512]{1,0:T(8,128)(2,1)S(1)} %collective-permute-done.3), channel_id=1, source_target_pairs={{0,30},{2,0},{4,2},{6,4},{8,6},{10,8},{12,10},{14,12},{16,14},{18,... | collective-permute-start | bytes 786440 | tf_op jit(solution)/shard_map/ppermute | solution.py:77
  55.9 98.0 %all-gather.9.cloned.1.call-done = bf16[1,4096,1536]{2,1,0:T(8,128)(2,1)} async-done(((bf16[1,256,1536]{2,1,0:T(8,128)(2,1)}), bf16[1,4096,1536]{2,1,0:T(8,128)(2,1)}) %all-gather.9.cloned.1.call-update) | async-done | bytes 12582928 | tf_op jit(solution)/shard_map/all_gather | solution.py:36
  153.9 7.1 %fusion.24 = f32[256,1536]{1,0:T(8,128)S(1)} fusion(bf16[256,4096]{1,0:T(8,128)(2,1)} %all-gather.5.cloned.1.call-done, bf16[1,4096,1536]{2,1,0:T(8,128)(2,1)} %all-gather.9.cloned.1.call-done), kind=kOutput, calls=%fused_computation.40 | convolution fusion | flops 3221225472 | bytes 16252928 | tf_op jit(solution)/shard_map/dot_general | solution.py:39
  162.3 2.2 broadcast_in_dim.17
  166.7 2.7 collective-permute-start.7
  169.4 83.3 %all-reduce.2.cloned.1.call-done = f32[64,1536]{1,0:T(8,128)} async-done(((f32[64,1536]{1,0:T(8,128)}), f32[64,1536]{1,0:T(8,128)}) %all-reduce.2.cloned.1.call-update) | async-done | bytes 393232 | tf_op jit(solution)/shard_map/psum | solution.py:46
  252.7 1.7 negate_bitcast_fusion.1
  254.4 3.7 %all_gather.15 = bf16[64,3072]{1,0:T(8,128)(2,1)S(1)} all-gather(bf16[64,1536]{1,0:T(8,128)(2,1)S(1)} %get-tuple-element.5), channel_id=1, replica_groups=mesh['dom'=8,'row'=16,'col'=2] {'col'}, dimensions={1}, use_global_device_ids=true | all-gather | bytes 589824 | tf_op jit(solution)/shard_map/all_gather | solution.py:52
  258.0 2.4 collective-permute-start.9
  263.5 2.3 collective-permute-done.9
  265.8 5.5 %collective-permute-start.11 = (bf16[256,512]{1,0:T(8,128)(2,1)S(1)}, bf16[256,512]{1,0:T(8,128)(2,1)S(1)}, u32[]{:S(2)}, u32[]{:S(2)}) collective-permute-start(bf16[256,512]{1,0:T(8,128)(2,1)S(1)} %collective-permute-done.9), channel_id=1, source_target_pairs={{0,30},{2,0},{4,2},{6,4},{8,6},{10,8},{12,10},{14,12},{16,14},{18,... | collective-permute-start | bytes 786440 | tf_op jit(solution)/shard_map/ppermute | solution.py:77
  273.3 2.6 copy.13
  275.9 6.3 %all-to-all-start = ((bf16[256,16,192]{0,2,1:T(8,128)(2,1)}), bf16[256,16,192]{0,2,1:T(8,128)(2,1)S(1)}, u32[]{:S(2)}, u32[]{:S(2)}) async-start(bf16[256,16,192]{0,2,1:T(8,128)(2,1)} %bitcast.36), calls=%async_computation | async-start | bytes 3145728 | tf_op jit(solution)/shard_map/all_to_all | solution.py:57
  282.9 4.7 %collective-permute-start.13 = (bf16[256,512]{1,0:T(8,128)(2,1)S(1)}, bf16[256,512]{1,0:T(8,128)(2,1)S(1)}, u32[]{:S(2)}, u32[]{:S(2)}) collective-permute-start(bf16[256,512]{1,0:T(8,128)(2,1)S(1)} %collective-permute-done.11), channel_id=1, source_target_pairs={{0,30},{2,0},{4,2},{6,4},{8,6},{10,8},{12,10},{14,12},{16,14},{18,... | collective-permute-start | bytes 786440 | tf_op jit(solution)/shard_map/ppermute | solution.py:77
  289.8 15.8 %collective-permute-done.13 = bf16[256,512]{1,0:T(8,128)(2,1)S(1)} collective-permute-done((bf16[256,512]{1,0:T(8,128)(2,1)S(1)}, bf16[256,512]{1,0:T(8,128)(2,1)S(1)}, u32[]{:S(2)}, u32[]{:S(2)}) %collective-permute-start.13) | collective-permute-done | bytes 262176 | tf_op jit(solution)/shard_map/ppermute | solution.py:77
  305.6 5.5 %collective-permute-start.15 = (bf16[256,512]{1,0:T(8,128)(2,1)S(1)}, bf16[256,512]{1,0:T(8,128)(2,1)S(1)}, u32[]{:S(2)}, u32[]{:S(2)}) collective-permute-start(bf16[256,512]{1,0:T(8,128)(2,1)S(1)} %collective-permute-done.13), channel_id=1, source_target_pairs={{0,30},{2,0},{4,2},{6,4},{8,6},{10,8},{12,10},{14,12},{16,14},{18,... | collective-permute-start | bytes 786440 | tf_op jit(solution)/shard_map/ppermute | solution.py:77
  311.1 1.7 constant_dynamic-update-slice_fusion.4
  315.6 6.2 %collective-permute-done.16 = bf16[256,512]{1,0:T(8,128)(2,1)S(1)} collective-permute-done((bf16[256,512]{1,0:T(8,128)(2,1)S(1)}, bf16[256,512]{1,0:T(8,128)(2,1)S(1)}, u32[]{:S(2)}, u32[]{:S(2)}) %collective-permute-start.16) | collective-permute-done | bytes 262176 | tf_op jit(solution)/shard_map/ppermute | solution.py:72
  323.7 8.8 %fusion.11 = bf16[192,2048]{1,0:T(8,128)(2,1)S(1)} fusion(f32[192,2048]{1,0:T(8,128)} %fusion.16, bf16[4096,192]{0,1:T(8,128)(2,1)S(1)} %bitcast.38, bf16[4096,512]{1,0:T(8,128)(2,1)} %constant_dynamic-update-slice_fusion, bf16[4096,1536]{1,0:T(8,128)(2,1)} %bitcast.42, bf16[192,512]{1,0:T(8,128)(2,1)S(1)} %bitcast.45, bf16[192,1536]{1,0:T(8,128)(2,1)} %bitcast.44), kind=kOutput, calls=%fused_computation.8 | convolution fusion | flops 3257532416 | bytes 21495808 | tf_op jit(solution)/shard_map/dot_general | solution.py:14
  (68 shorter events, 24.2 us)
Async XLA Ops:
  7.2 48.7 %all-gather.5.cloned.1.call-start = ((), (), s32[]{:S(2)}) async-start(), calls=%async_computation.1 | async-start | bytes 3145728 | tf_op jit(solution)/shard_map/all_gather | solution.py:40
  7.2 25.5 %collective-permute-start.1 = (bf16[256,2048]{1,0:T(8,128)(2,1)}, bf16[256,2048]{1,0:T(8,128)(2,1)S(1)}, u32[]{:S(2)}, u32[]{:S(2)}) collective-permute-start(bf16[256,2048]{1,0:T(8,128)(2,1)} %bitcast.43), channel_id=1, source_target_pairs={{32,0},{64,32},{96,64},{128,96},{160,128},{192,160},{224,192},{33,... | collective-permute-start | bytes 3145736 | tf_op jit(solution)/shard_map/ppermute | solution.py:10
  33.8 120.1 %all-gather.9.cloned.1.call-start = ((), (), s32[]{:S(2)}) async-start(), calls=%async_computation.4 | async-start | bytes 13369344 | tf_op jit(solution)/shard_map/all_gather | solution.py:36
  34.5 218.1 %all-reduce.2.cloned.1.call-start = ((), (), s32[]{:S(2)}) async-start(), calls=%async_computation.2 | async-start | bytes 786432 | tf_op jit(solution)/shard_map/psum | solution.py:46
  34.6 12.2 %collective-permute-start.2 = (bf16[256,512]{1,0:T(8,128)(2,1)}, bf16[256,512]{1,0:T(8,128)(2,1)S(1)}, u32[]{:S(2)}, u32[]{:S(2)}) collective-permute-start(bf16[256,512]{1,0:T(8,128)(2,1)} %bitcast.39), channel_id=1, source_target_pairs={{0,2},{2,4},{4,6},{6,8},{8,10},{10,12},{12,14},{14,16},{16,18},{18... | collective-permute-start | bytes 786440 | tf_op jit(solution)/shard_map/ppermute | solution.py:72
  37.7 12.4 %collective-permute-start.3 = (bf16[256,512]{1,0:T(8,128)(2,1)}, bf16[256,512]{1,0:T(8,128)(2,1)S(1)}, u32[]{:S(2)}, u32[]{:S(2)}) collective-permute-start(bf16[256,512]{1,0:T(8,128)(2,1)} %bitcast.40), channel_id=1, source_target_pairs={{0,30},{2,0},{4,2},{6,4},{8,6},{10,8},{12,10},{14,12},{16,14},{18,... | collective-permute-start | bytes 786440 | tf_op jit(solution)/shard_map/ppermute | solution.py:77
  41.5 6.4 %collective-permute-start = (bf16[64,256]{1,0:T(8,128)(2,1)}, bf16[64,256]{1,0:T(8,128)(2,1)S(1)}, u32[]{:S(2)}, u32[]{:S(2)}) collective-permute-start(bf16[64,256]{1,0:T(8,128)(2,1)} %bitcast.46), channel_id=1, source_target_pairs={{32,0},{64,32},{96,64},{128,96},{160,128},{192,160},{224,192},{33,... | collective-permute-start | bytes 98312 | tf_op jit(solution)/shard_map/ppermute | solution.py:10
  46.8 9.0 %collective-permute-start.4 = (bf16[256,512]{1,0:T(8,128)(2,1)S(1)}, bf16[256,512]{1,0:T(8,128)(2,1)S(1)}, u32[]{:S(2)}, u32[]{:S(2)}) collective-permute-start(bf16[256,512]{1,0:T(8,128)(2,1)S(1)} %collective-permute-done.2), channel_id=1, source_target_pairs={{0,2},{2,4},{4,6},{6,8},{8,10},{10,12},{12,14},{14,16},{16,18},{18... | collective-permute-start | bytes 786440 | tf_op jit(solution)/shard_map/ppermute | solution.py:72
  50.1 110.9 %copy-start.2 = (bf16[1,64,1536]{2,1,0:T(8,128)(2,1)S(1)}, bf16[1,64,1536]{2,1,0:T(8,128)(2,1)}, u32[]{:S(2)}) copy-start(bf16[1,64,1536]{2,1,0:T(8,128)(2,1)} %param.13) | copy-start | bytes 589828
  50.1 223.3 %all-gather.7.cloned.1.call-start = ((), (), s32[]{:S(2)}) async-start(), calls=%async_computation.3 | async-start | bytes 2359296 | tf_op jit(solution)/shard_map/all_gather | solution.py:51
  50.1 116.6 %collective-permute-start.5 = (bf16[256,512]{1,0:T(8,128)(2,1)S(1)}, bf16[256,512]{1,0:T(8,128)(2,1)S(1)}, u32[]{:S(2)}, u32[]{:S(2)}) collective-permute-start(bf16[256,512]{1,0:T(8,128)(2,1)S(1)} %collective-permute-done.3), channel_id=1, source_target_pairs={{0,30},{2,0},{4,2},{6,4},{8,6},{10,8},{12,10},{14,12},{16,14},{18,... | collective-permute-start | bytes 786440 | tf_op jit(solution)/shard_map/ppermute | solution.py:77
  55.8 113.6 %collective-permute-start.6 = (bf16[256,512]{1,0:T(8,128)(2,1)S(1)}, bf16[256,512]{1,0:T(8,128)(2,1)S(1)}, u32[]{:S(2)}, u32[]{:S(2)}) collective-permute-start(bf16[256,512]{1,0:T(8,128)(2,1)S(1)} %collective-permute-done.4), channel_id=1, source_target_pairs={{0,2},{2,4},{4,6},{6,8},{8,10},{10,12},{12,14},{14,16},{16,18},{18... | collective-permute-start | bytes 786440 | tf_op jit(solution)/shard_map/ppermute | solution.py:72
  162.3 98.2 %copy-start.5 = (bf16[1,64,512]{2,1,0:T(8,128)(2,1)S(1)}, bf16[1,64,512]{2,1,0:T(8,128)(2,1)}, u32[]{:S(2)}) copy-start(bf16[1,64,512]{2,1,0:T(8,128)(2,1)} %param.14) | copy-start | bytes 196612
  166.7 91.4 %collective-permute-start.7 = (bf16[256,512]{1,0:T(8,128)(2,1)S(1)}, bf16[256,512]{1,0:T(8,128)(2,1)S(1)}, u32[]{:S(2)}, u32[]{:S(2)}) collective-permute-start(bf16[256,512]{1,0:T(8,128)(2,1)S(1)} %collective-permute-done.5), channel_id=1, source_target_pairs={{0,30},{2,0},{4,2},{6,4},{8,6},{10,8},{12,10},{14,12},{16,14},{18,... | collective-permute-start | bytes 786440 | tf_op jit(solution)/shard_map/ppermute | solution.py:77
  169.4 92.8 %collective-permute-start.8 = (bf16[256,512]{1,0:T(8,128)(2,1)S(1)}, bf16[256,512]{1,0:T(8,128)(2,1)S(1)}, u32[]{:S(2)}, u32[]{:S(2)}) collective-permute-start(bf16[256,512]{1,0:T(8,128)(2,1)S(1)} %collective-permute-done.6), channel_id=1, source_target_pairs={{0,2},{2,4},{4,6},{6,8},{8,10},{10,12},{12,14},{14,16},{16,18},{18... | collective-permute-start | bytes 786440 | tf_op jit(solution)/shard_map/ppermute | solution.py:72
  258.0 7.8 %collective-permute-start.9 = (bf16[256,512]{1,0:T(8,128)(2,1)S(1)}, bf16[256,512]{1,0:T(8,128)(2,1)S(1)}, u32[]{:S(2)}, u32[]{:S(2)}) collective-permute-start(bf16[256,512]{1,0:T(8,128)(2,1)S(1)} %collective-permute-done.7), channel_id=1, source_target_pairs={{0,30},{2,0},{4,2},{6,4},{8,6},{10,8},{12,10},{14,12},{16,14},{18,... | collective-permute-start | bytes 786440 | tf_op jit(solution)/shard_map/ppermute | solution.py:77
  262.1 10.5 %collective-permute-start.10 = (bf16[256,512]{1,0:T(8,128)(2,1)S(1)}, bf16[256,512]{1,0:T(8,128)(2,1)S(1)}, u32[]{:S(2)}, u32[]{:S(2)}) collective-permute-start(bf16[256,512]{1,0:T(8,128)(2,1)S(1)} %collective-permute-done.8), channel_id=1, source_target_pairs={{0,2},{2,4},{4,6},{6,8},{8,10},{10,12},{12,14},{14,16},{16,18},{18... | collective-permute-start | bytes 786440 | tf_op jit(solution)/shard_map/ppermute | solution.py:72
  265.8 17.1 %collective-permute-start.11 = (bf16[256,512]{1,0:T(8,128)(2,1)S(1)}, bf16[256,512]{1,0:T(8,128)(2,1)S(1)}, u32[]{:S(2)}, u32[]{:S(2)}) collective-permute-start(bf16[256,512]{1,0:T(8,128)(2,1)S(1)} %collective-permute-done.9), channel_id=1, source_target_pairs={{0,30},{2,0},{4,2},{6,4},{8,6},{10,8},{12,10},{14,12},{16,14},{18,... | collective-permute-start | bytes 786440 | tf_op jit(solution)/shard_map/ppermute | solution.py:77
  272.6 15.7 %collective-permute-start.12 = (bf16[256,512]{1,0:T(8,128)(2,1)S(1)}, bf16[256,512]{1,0:T(8,128)(2,1)}, u32[]{:S(2)}, u32[]{:S(2)}) collective-permute-start(bf16[256,512]{1,0:T(8,128)(2,1)S(1)} %collective-permute-done.10), channel_id=1, source_target_pairs={{0,2},{2,4},{4,6},{6,8},{8,10},{10,12},{12,14},{14,16},{16,18},{18... | collective-permute-start | bytes 786440 | tf_op jit(solution)/shard_map/ppermute | solution.py:72
  275.9 47.6 %all-to-all-start = ((bf16[256,16,192]{0,2,1:T(8,128)(2,1)}), bf16[256,16,192]{0,2,1:T(8,128)(2,1)S(1)}, u32[]{:S(2)}, u32[]{:S(2)}) async-start(bf16[256,16,192]{0,2,1:T(8,128)(2,1)} %bitcast.36), calls=%async_computation | async-start | bytes 3145728 | tf_op jit(solution)/shard_map/all_to_all | solution.py:57
  282.9 22.6 %collective-permute-start.13 = (bf16[256,512]{1,0:T(8,128)(2,1)S(1)}, bf16[256,512]{1,0:T(8,128)(2,1)S(1)}, u32[]{:S(2)}, u32[]{:S(2)}) collective-permute-start(bf16[256,512]{1,0:T(8,128)(2,1)S(1)} %collective-permute-done.11), channel_id=1, source_target_pairs={{0,30},{2,0},{4,2},{6,4},{8,6},{10,8},{12,10},{14,12},{16,14},{18,... | collective-permute-start | bytes 786440 | tf_op jit(solution)/shard_map/ppermute | solution.py:77
  288.3 24.4 %collective-permute-start.14 = (bf16[256,512]{1,0:T(8,128)(2,1)}, bf16[256,512]{1,0:T(8,128)(2,1)S(1)}, u32[]{:S(2)}, u32[]{:S(2)}) collective-permute-start(bf16[256,512]{1,0:T(8,128)(2,1)} %collective-permute-done.12), channel_id=1, source_target_pairs={{0,2},{2,4},{4,6},{6,8},{8,10},{10,12},{12,14},{14,16},{16,18},{18... | collective-permute-start | bytes 786440 | tf_op jit(solution)/shard_map/ppermute | solution.py:72
  305.6 9.4 %collective-permute-start.15 = (bf16[256,512]{1,0:T(8,128)(2,1)S(1)}, bf16[256,512]{1,0:T(8,128)(2,1)S(1)}, u32[]{:S(2)}, u32[]{:S(2)}) collective-permute-start(bf16[256,512]{1,0:T(8,128)(2,1)S(1)} %collective-permute-done.13), channel_id=1, source_target_pairs={{0,30},{2,0},{4,2},{6,4},{8,6},{10,8},{12,10},{14,12},{16,14},{18,... | collective-permute-start | bytes 786440 | tf_op jit(solution)/shard_map/ppermute | solution.py:77
  312.8 9.1 %collective-permute-start.16 = (bf16[256,512]{1,0:T(8,128)(2,1)S(1)}, bf16[256,512]{1,0:T(8,128)(2,1)S(1)}, u32[]{:S(2)}, u32[]{:S(2)}) collective-permute-start(bf16[256,512]{1,0:T(8,128)(2,1)S(1)} %collective-permute-done.14), channel_id=1, source_target_pairs={{0,2},{2,4},{4,6},{6,8},{8,10},{10,12},{12,14},{14,16},{16,18},{18... | collective-permute-start | bytes 786440 | tf_op jit(solution)/shard_map/ppermute | solution.py:72
  (5 other events, 126.1 us)
Sparse Core Ops, SparseCore 0:
  33.9 21.8 all-gather.4
  58.3 95.5 all-gather.8
  157.7 94.9 all-reduce.1
  254.9 16.5 all-gather.6
